TPU v7x, 32 devices: a whole 2x2x4 slice. The times are simulated.
32 devices in a mesh: node: 8 (over z, y), local: 4 (over x, core).
Axes of the slice: x: 2, y: 2, z: 4, core: 2. Of those that a mesh axis runs over, the one named last changes fastest.
Arguments:
- tokens: bfloat16 [4096, 7168], P(('node', 'local')), may hold values from -6 to 6
- out_grad: bfloat16 [4096, 7168], P(('node', 'local')), may hold values from -6 to 6
- route_ids: int32 [4096, 1], P(('node', 'local')), may hold values from 0 to 7; in each aligned block of 128 rows (0 to 127, 128 to 255, ...) at most 24 rows name the same one
- route_weights: bfloat16 [4096, 1], P(('node', 'local')), may hold values from 0.049804688 to 1
- gate_proj: bfloat16 [8, 7168, 2048], P('node', None, 'local'), may hold values from -0.0625 to 0.0625
- up_proj: bfloat16 [8, 7168, 2048], P('node', None, 'local'), may hold values from -0.0625 to 0.0625
- down_proj: bfloat16 [8, 2048, 7168], P('node', 'local'), may hold values from -0.125 to 0.125
Outputs:
- grad_tokens: bfloat16 [4096, 7168], P(('node', 'local'))
- grad_routes: float32 [4096, 1], P(('node', 'local'))
- grad_gate: bfloat16 [8, 7168, 2048], P('node', None, 'local')
- grad_up: bfloat16 [8, 7168, 2048], P('node', None, 'local')
- grad_down: bfloat16 [8, 2048, 7168], P('node', 'local')
Inputs may be any that keep to these rules, and one draw needn't show every extreme that they name: `route_ids`: the 1 ids of a token are distinct; among the 128 tokens of one block no id appears more than 24 times, and in every draw some block names some id exactly 24 times. Every id is named somewhere.
All inputs are finite; a program needn't handle non-finite values.
Results may differ from a plain program's by a relative error of at most 0.0095.
Values may be sent and summed in bfloat16 or wider, within the bound.
A program may use at most 384 MiB of HBM per device.

v0:
```python
import jax
import jax.numpy as jnp
from jax import lax
from jax.sharding import PartitionSpec as P


def slot_tables(route_ids, experts, capacity):
    tok_count, top_count = route_ids.shape
    flat_ids = route_ids.reshape(tok_count * top_count)
    route_order = jnp.arange(tok_count * top_count, dtype=jnp.int32)
    same_ids = (flat_ids[:, None] == flat_ids[None, :]) & (
        route_order[None, :] < route_order[:, None]
    )
    rank_ids = jnp.sum(same_ids.astype(jnp.int32), axis=1)
    slot_index = flat_ids * capacity + rank_ids
    slot_lines = jnp.arange(experts * capacity, dtype=jnp.int32)
    by_route = slot_lines[:, None] == slot_index[None, :]
    by_token = jnp.any(by_route.reshape(experts * capacity, tok_count, top_count), axis=2)
    return (by_route, by_token)


def shards(tokens, out_grad, route_ids, route_weights, gate_proj, up_proj, down_proj):
    node_count = lax.axis_size("node")
    local_count = lax.axis_size("local")
    tok_count, top_count = route_ids.shape
    model_width = tokens.shape[1]
    capacity = max(2, 3 * tok_count * top_count // (2 * node_count))
    by_route, by_token = slot_tables(route_ids, node_count, capacity)
    token_mask = by_token.astype(jnp.bfloat16)
    send_x = jnp.dot(token_mask, tokens, preferred_element_type=jnp.float32).astype(jnp.bfloat16)
    send_dy = jnp.dot(token_mask, out_grad, preferred_element_type=jnp.float32).astype(jnp.bfloat16)
    weight_line = route_weights.reshape(1, tok_count * top_count).astype(jnp.float32)
    send_g = jnp.sum(jnp.where(by_route, weight_line, 0.0), axis=1).astype(jnp.bfloat16)

    def spread_copies(array):
        tail = array.shape[1:]
        shaped = array.reshape((node_count, 1, capacity) + tail)
        wide = jnp.broadcast_to(shaped, (node_count, local_count, capacity) + tail)
        return wide.reshape((node_count * local_count * capacity,) + tail)

    rows_x, rows_dy, rows_g = (
        lax.all_to_all(
            spread_copies(send_x), ("node", "local"), split_axis=0, concat_axis=0, tiled=True
        ),
        lax.all_to_all(
            spread_copies(send_dy), ("node", "local"), split_axis=0, concat_axis=0, tiled=True
        ),
        lax.all_to_all(
            spread_copies(send_g), ("node", "local"), split_axis=0, concat_axis=0, tiled=True
        ),
    )
    gate_w = gate_proj[0]
    up_w = up_proj[0]
    down_w = down_proj[0]
    pre_gate = jnp.dot(rows_x, gate_w, preferred_element_type=jnp.float32)
    pre_up = jnp.dot(rows_x, up_w, preferred_element_type=jnp.float32)
    gate_sigmoid = jax.nn.sigmoid(pre_gate)
    gate_silu = pre_gate * gate_sigmoid
    activated = (gate_silu * pre_up).astype(jnp.bfloat16)
    back_proj = lax.dot_general(
        rows_dy, down_w, (((1,), (1,)), ((), ())), preferred_element_type=jnp.float32
    )
    gate_scale = rows_g.astype(jnp.float32)[:, None]
    grad_act = gate_scale * back_proj
    grad_pregate = (
        grad_act * pre_up * gate_sigmoid * (1.0 + pre_gate * (1.0 - gate_sigmoid))
    ).astype(jnp.bfloat16)
    grad_preup = (grad_act * gate_silu).astype(jnp.bfloat16)
    scaled = (gate_scale * rows_dy.astype(jnp.float32)).astype(jnp.bfloat16)
    part_g = jnp.sum(activated.astype(jnp.float32) * back_proj, axis=1)
    part_x = lax.dot_general(
        grad_pregate, gate_w, (((1,), (1,)), ((), ())), preferred_element_type=jnp.float32
    )
    part_x = part_x + lax.dot_general(
        grad_preup, up_w, (((1,), (1,)), ((), ())), preferred_element_type=jnp.float32
    )
    rows_first = (((0,), (0,)), ((), ()))
    grad_gate = lax.dot_general(
        rows_x, grad_pregate, rows_first, preferred_element_type=jnp.float32
    ).astype(jnp.bfloat16)
    grad_up = lax.dot_general(
        rows_x, grad_preup, rows_first, preferred_element_type=jnp.float32
    ).astype(jnp.bfloat16)
    grad_down = lax.dot_general(
        activated, scaled, rows_first, preferred_element_type=jnp.float32
    ).astype(jnp.bfloat16)
    got_x, got_g = (
        lax.all_to_all(
            part_x.astype(jnp.bfloat16), ("node", "local"), split_axis=0, concat_axis=0, tiled=True
        ),
        lax.all_to_all(
            part_g.astype(jnp.bfloat16), ("node", "local"), split_axis=0, concat_axis=0, tiled=True
        ),
    )
    back_x = jnp.sum(
        got_x.reshape(node_count, local_count, capacity, model_width).astype(jnp.float32), axis=1
    )
    back_x = back_x.reshape(node_count * capacity, model_width)
    back_g = jnp.sum(got_g.reshape(node_count, local_count, capacity).astype(jnp.float32), axis=1)
    back_g = back_g.reshape(node_count * capacity)
    grad_tokens = jnp.dot(
        by_token.astype(jnp.float32).T,
        back_x,
        precision=lax.Precision.HIGHEST,
        preferred_element_type=jnp.float32,
    ).astype(jnp.bfloat16)
    grad_routes = jnp.sum(jnp.where(by_route, back_g[:, None], 0.0), axis=0).reshape(
        tok_count, top_count
    )
    return (
        grad_tokens,
        grad_routes,
        grad_gate.reshape(gate_proj.shape),
        grad_up.reshape(up_proj.shape),
        grad_down.reshape(down_proj.shape),
    )


def solution(mesh):
    placed = (
        P(("node", "local"), None),
        P(("node", "local"), None),
        P(("node", "local"), None),
        P(("node", "local"), None),
        P("node", None, "local"),
        P("node", None, "local"),
        P("node", "local", None),
    )
    return jax.shard_map(
        shards,
        mesh=mesh,
        in_specs=placed,
        out_specs=(
            P(("node", "local"), None),
            P(("node", "local"), None),
            P("node", None, "local"),
            P("node", None, "local"),
            P("node", "local", None),
        ),
        check_vma=False,
    )
```

profile of v0, /device:TPU:0, one launch (start us, length us, event | category | flops | bytes accessed | tf_op | source)
XLA Modules:
  0.0 848.9 jit_solution(14052419065888040372)
XLA Ops:
  2.3 2.4 convolution_convert_fusion.2
  4.7 7.3 broadcast_in_dim.54
  12.0 7.4 all-to-all-start.2
  19.4 2.4 convolution_convert_fusion.3
  21.8 241.5 %all-to-all-done.2 = bf16[32,24,7168]{2,1,0:T(8,128)(2,1)} async-done(((bf16[32,24,7168]{2,1,0:T(8,128)(2,1)}), bf16[32,24,7168]{2,1,0:T(8,128)(2,1)}, u32[]{:S(2)}, u32[]{:S(2)}) %all-to-all-start.2) | async-done | bytes 11010080 | tf_op jit(solution)/shard_map/all_to_all | solution.py:42
  263.3 7.3 broadcast_in_dim.52
  270.6 3.9 all-to-all-start.1
  274.5 12.4 %fusion.8 = f32[768,512]{0,1:T(8,128)S(1)} fusion(bf16[768,7168]{1,0:T(8,128)(2,1)} %bitcast.9, bf16[1,7168,512]{2,1,0:T(8,128)(2,1)} %param.11), kind=kOutput, calls=%fused_computation.16 | convolution fusion | flops 5637144576 | bytes 19922944 | tf_op jit(solution)/shard_map/dot_general | solution.py:55
  287.0 12.4 %fusion.11 = f32[768,512]{0,1:T(8,128)S(1)} fusion(bf16[768,7168]{1,0:T(8,128)(2,1)} %bitcast.9, bf16[1,7168,512]{2,1,0:T(8,128)(2,1)} %param.12), kind=kOutput, calls=%fused_computation.19 | convolution fusion | flops 5637144576 | bytes 19922944 | tf_op jit(solution)/shard_map/dot_general | solution.py:56
  299.4 219.2 %all-to-all-done.1 = bf16[32,24,7168]{2,1,0:T(8,128)(2,1)} async-done(((bf16[32,24,7168]{2,1,0:T(8,128)(2,1)}), bf16[32,24,7168]{2,1,0:T(8,128)(2,1)}, u32[]{:S(2)}, u32[]{:S(2)}) %all-to-all-start.1) | async-done | bytes 11010080 | tf_op jit(solution)/shard_map/all_to_all | solution.py:45
  518.6 12.4 %multiply_reduce_fusion = (bf16[768]{0:T(1024)(128)(2,1)S(1)}, bf16[768,512]{0,1:T(8,128)(2,1)}, f32[768,512]{0,1:T(8,128)}) fusion(f32[768,512]{0,1:T(8,128)S(1)} %fusion.11, f32[768,512]{0,1:T(8,128)S(1)} %fusion.8, bf16[768,7168]{1,0:T(8,128)(2,1)} %bitcast.5, bf16[1,512,7168]{2,1,0:T(8,128)(2,1)} %param.13), kind=kOutput, calls=%fused_computation.23 | convolution fusion | flops 5640682496 | bytes 23856640 | tf_op jit(solution)/shard_map/dot_general | solution.py:60
  531.7 2.5 all-to-all-start.4
  534.3 7.1 all-to-all-done.4
  542.2 8.8 %all_to_all.48 = bf16[32,24,1]{1,2,0:T(2,128)(2,1)S(1)} all-to-all(bf16[32,24,1]{1,2,0:T(2,128)(2,1)S(1)} %copy.17), channel_id=1, replica_groups=mesh['node'=8,'local'=4] {'node','local'}, dimensions={0} | all-to-all | bytes 3072 | tf_op jit(solution)/shard_map/all_to_all | solution.py:48
  551.2 3.1 multiply_convert_fusion.7
  554.2 13.8 %fusion.6 = f32[768,7168]{1,0:T(8,128)} fusion(bf16[768,512]{0,1:T(8,128)(2,1)S(1)} %get-tuple-element.10, bf16[1,7168,512]{2,1,0:T(8,128)(2,1)} %param.11), kind=kOutput, calls=%fused_computation.14 | convolution fusion | flops 5637144576 | bytes 30146560 | tf_op jit(solution)/shard_map/dot_general | solution.py:71
  568.0 17.2 %add_convert_fusion = bf16[768,7168]{1,0:T(8,128)(2,1)} fusion(f32[768,7168]{1,0:T(8,128)} %fusion.6, bf16[768,512]{0,1:T(8,128)(2,1)S(1)} %copy-done.5, bf16[1,7168,512]{2,1,0:T(8,128)(2,1)} %param.12), kind=kOutput, calls=%fused_computation.2 | convolution fusion | flops 5648154624 | bytes 41156608 | tf_op jit(solution)/shard_map/dot_general | solution.py:74
  585.3 4.0 all-to-all-start.3
  589.3 12.3 %fusion.5 = bf16[1,7168,512]{2,1,0:T(8,128)(2,1)} fusion(bf16[768,7168]{1,0:T(8,128)(2,1)} %bitcast.9, bf16[768,512]{0,1:T(8,128)(2,1)S(1)} %copy-done.5), kind=kOutput, calls=%fused_computation.10 | convolution fusion | flops 5640814592 | bytes 19136512 | tf_op jit(solution)/shard_map/dot_general | solution.py:81
  601.5 12.2 %fusion.4 = bf16[1,7168,512]{2,1,0:T(8,128)(2,1)} fusion(bf16[768,7168]{1,0:T(8,128)(2,1)} %bitcast.9, bf16[768,512]{0,1:T(8,128)(2,1)S(1)} %copy-done.4), kind=kOutput, calls=%fused_computation.9 | convolution fusion | flops 5640814592 | bytes 19136512 | tf_op jit(solution)/shard_map/dot_general | solution.py:78
  613.8 12.3 %fusion.3 = bf16[1,512,7168]{2,1,0:T(8,128)(2,1)} fusion(bf16[768,512]{0,1:T(8,128)(2,1)S(1)} %copy-done.7, bf16[768,7168]{1,0:T(8,128)(2,1)} %bitcast.5, f32[768]{0:T(1024)S(1)} %reshape.111), kind=kOutput, calls=%fused_computation.8 | convolution fusion | flops 5657329664 | bytes 19139584 | tf_op jit(solution)/shard_map/dot_general | solution.py:84
  626.0 207.3 %all-to-all-done.3 = bf16[32,24,7168]{2,1,0:T(8,128)(2,1)} async-done(((bf16[32,24,7168]{2,1,0:T(8,128)(2,1)}), bf16[32,24,7168]{2,1,0:T(8,128)(2,1)}, u32[]{:S(2)}, u32[]{:S(2)}) %all-to-all-start.3) | async-done | bytes 11010080 | tf_op jit(solution)/shard_map/all_to_all | solution.py:88
  833.3 9.3 %convert_reduce_fusion = f32[8,24,7168]{2,1,0:T(8,128)} fusion(bf16[32,24,7168]{2,1,0:T(8,128)(2,1)} %all-to-all-done.3), kind=kLoop, calls=%fused_computation | loop fusion | flops 9633792 | bytes 16515072 | tf_op jit(solution)/shard_map/reduce_sum | solution.py:95
  842.6 6.4 convolution_convert_fusion.4
  (29 shorter events, 3.4 us)
Async XLA Ops:
  0.6 1.7 copy-start
  12.0 7.4 copy-start.2
  12.0 251.3 %all-to-all-start.2 = ((bf16[32,24,7168]{2,1,0:T(8,128)(2,1)}), bf16[32,24,7168]{2,1,0:T(8,128)(2,1)}, u32[]{:S(2)}, u32[]{:S(2)}) async-start(bf16[32,24,7168]{2,1,0:T(8,128)(2,1)} %bitcast.55), calls=%async_computation.2 | async-start | bytes 22020096 | tf_op jit(solution)/shard_map/all_to_all | solution.py:42
  270.6 248.0 %all-to-all-start.1 = ((bf16[32,24,7168]{2,1,0:T(8,128)(2,1)}), bf16[32,24,7168]{2,1,0:T(8,128)(2,1)}, u32[]{:S(2)}, u32[]{:S(2)}) async-start(bf16[32,24,7168]{2,1,0:T(8,128)(2,1)} %bitcast.54), calls=%async_computation.1 | async-start | bytes 22020096 | tf_op jit(solution)/shard_map/all_to_all | solution.py:45
  518.6 15.7 %copy-start.6 = (bf16[128,1]{0,1:T(2,128)(2,1)S(1)}, bf16[128,1]{0,1:T(2,128)(2,1)}, u32[]{:S(2)}) copy-start(bf16[128,1]{0,1:T(2,128)(2,1)} %param.10) | copy-start | bytes 772
  531.7 9.6 %all-to-all-start.4 = ((bf16[32,24,1]{1,2,0:T(2,128)(2,1)}), bf16[32,24,1]{1,2,0:T(2,128)(2,1)S(1)}, u32[]{:S(2)}, u32[]{:S(2)}) async-start(bf16[32,24,1]{1,2,0:T(2,128)(2,1)} %convert_element_type.133), calls=%async_computation.4 | async-start | bytes 32768 | tf_op jit(solution)/shard_map/all_to_all | solution.py:91
  554.2 13.8 %copy-start.3 = (bf16[768,512]{0,1:T(8,128)(2,1)}, bf16[768,512]{0,1:T(8,128)(2,1)S(1)}, u32[]{:S(2)}) copy-start(bf16[768,512]{0,1:T(8,128)(2,1)S(1)} %get-tuple-element.10) | copy-start | bytes 2359300
  554.2 13.8 %copy-start.5 = (bf16[768,512]{0,1:T(8,128)(2,1)S(1)}, bf16[768,512]{0,1:T(8,128)(2,1)}, u32[]{:S(2)}) copy-start(bf16[768,512]{0,1:T(8,128)(2,1)} %get-tuple-element.9) | copy-start | bytes 2359300
  585.3 248.0 %all-to-all-start.3 = ((bf16[32,24,7168]{2,1,0:T(8,128)(2,1)}), bf16[32,24,7168]{2,1,0:T(8,128)(2,1)}, u32[]{:S(2)}, u32[]{:S(2)}) async-start(bf16[32,24,7168]{2,1,0:T(8,128)(2,1)} %bitcast.57), calls=%async_computation.3 | async-start | bytes 22020096 | tf_op jit(solution)/shard_map/all_to_all | solution.py:88
  589.2 12.3 %copy-start.4 = (bf16[768,512]{0,1:T(8,128)(2,1)S(1)}, bf16[768,512]{0,1:T(8,128)(2,1)}, u32[]{:S(2)}) copy-start(bf16[768,512]{0,1:T(8,128)(2,1)} %copy-done.3) | copy-start | bytes 2359300
  601.5 12.2 %copy-start.7 = (bf16[768,512]{0,1:T(8,128)(2,1)S(1)}, bf16[768,512]{0,1:T(8,128)(2,1)}, u32[]{:S(2)}) copy-start(bf16[768,512]{0,1:T(8,128)(2,1)} %get-tuple-element.8) | copy-start | bytes 2359300
  833.3 15.6 %copy-start.1 = (bf16[128,7168]{1,0:T(8,128)(2,1)S(1)}, bf16[128,7168]{1,0:T(8,128)(2,1)}, u32[]{:S(2)}) copy-start(bf16[128,7168]{1,0:T(8,128)(2,1)} %param.7) | copy-start | bytes 5505028
where the time goes:
time: 850 us; the launch traced here: 849 us
  waiting for transfers between devices  675 us (79%)
  matrix products  116 us (14%)
  starting transfers between devices  17.8 us (2%)
  local copies, waits for them, and re-layouts  15.6 us (2%)
  other arithmetic  14.7 us (2%)
  blocking collectives  8.85 us (1%)
    all_to_all x1, waiting for transfers between devices, shards(): lax.all_to_all(spread_copies(send_x), ('node', 'local'), split_axis=0, co...  241 us
    all_to_all x1, waiting for transfers between devices, shards(): lax.all_to_all(spread_copies(send_dy), ('node', 'local'), split_axis=0, c...  219 us
    all_to_all x1, waiting for transfers between devices, shards(): lax.all_to_all(part_x.astype(jnp.bfloat16), ('node', 'local'), split_axis...  207 us
    dot_general x1, matrix products, shards(): lax.dot_general(grad_preup, up_w, (((1,), (1,)), ((), ())), preferred_ele...  17.2 us
  transfers between devices with their start and end apart: 4, of which 4 were waited for; matrix products, arithmetic and copies ran while one was open for 8% of the time, Pallas kernels for 0%

commit v1 on v0

v1 whole, which is shorter than its diff:
```python
import jax
import jax.numpy as jnp
from jax import lax
from jax.sharding import PartitionSpec as P

IN_PARTS = 2
OUT_PARTS = 2


def slot_tables(route_ids, experts, capacity):
    tok_count, top_count = route_ids.shape
    flat_ids = route_ids.reshape(tok_count * top_count)
    route_order = jnp.arange(tok_count * top_count, dtype=jnp.int32)
    same_ids = (flat_ids[:, None] == flat_ids[None, :]) & (
        route_order[None, :] < route_order[:, None]
    )
    rank_ids = jnp.sum(same_ids.astype(jnp.int32), axis=1)
    slot_index = flat_ids * capacity + rank_ids
    slot_lines = jnp.arange(experts * capacity, dtype=jnp.int32)
    by_route = slot_lines[:, None] == slot_index[None, :]
    by_token = jnp.any(by_route.reshape(experts * capacity, tok_count, top_count), axis=2)
    return (by_route, by_token)


def columns(array, part, parts):
    width = array.shape[1] // parts
    return array[:, part * width : (part + 1) * width]


def shards(tokens, out_grad, route_ids, route_weights, gate_proj, up_proj, down_proj):
    node_count = lax.axis_size("node")
    local_count = lax.axis_size("local")
    tok_count, top_count = route_ids.shape
    capacity = max(2, 3 * tok_count * top_count // (2 * node_count))
    by_route, by_token = slot_tables(route_ids, node_count, capacity)
    token_mask = by_token.astype(jnp.bfloat16)
    weight_line = route_weights.reshape(1, tok_count * top_count).astype(jnp.float32)
    send_g = jnp.sum(jnp.where(by_route, weight_line, 0.0), axis=1).astype(jnp.bfloat16)

    def spread(rows):
        near = lax.all_to_all(rows, "node", split_axis=0, concat_axis=0, tiled=True)
        return lax.all_gather(near, "local", axis=0, tiled=True)

    def collect(rows):
        near = lax.psum_scatter(rows, "local", scatter_dimension=0, tiled=True)
        return lax.all_to_all(near, "node", split_axis=0, concat_axis=0, tiled=True)

    def dispatch(array):
        return [
            spread(
                jnp.dot(
                    token_mask, columns(array, c, IN_PARTS), preferred_element_type=jnp.float32
                ).astype(jnp.bfloat16)
            )
            for c in range(IN_PARTS)
        ]

    rows_x = dispatch(tokens)
    rows_g = spread(send_g.reshape(node_count, capacity)).reshape(-1)
    rows_dy = dispatch(out_grad)
    gate_w = gate_proj[0]
    up_w = up_proj[0]
    down_w = down_proj[0]
    width = gate_w.shape[0] // IN_PARTS
    pre_gate = sum(
        jnp.dot(r, gate_w[c * width : (c + 1) * width], preferred_element_type=jnp.float32)
        for c, r in enumerate(rows_x)
    )
    pre_up = sum(
        jnp.dot(r, up_w[c * width : (c + 1) * width], preferred_element_type=jnp.float32)
        for c, r in enumerate(rows_x)
    )
    gate_sigmoid = jax.nn.sigmoid(pre_gate)
    gate_silu = pre_gate * gate_sigmoid
    activated = (gate_silu * pre_up).astype(jnp.bfloat16)
    columns_both = (((1,), (1,)), ((), ()))
    back_proj = sum(
        lax.dot_general(
            r, columns(down_w, c, IN_PARTS), columns_both, preferred_element_type=jnp.float32
        )
        for c, r in enumerate(rows_dy)
    )
    gate_scale = rows_g.astype(jnp.float32)[:, None]
    grad_act = gate_scale * back_proj
    grad_pregate = (
        grad_act * pre_up * gate_sigmoid * (1.0 + pre_gate * (1.0 - gate_sigmoid))
    ).astype(jnp.bfloat16)
    grad_preup = (grad_act * gate_silu).astype(jnp.bfloat16)
    part_g = jnp.sum(activated.astype(jnp.float32) * back_proj, axis=1)
    width = gate_w.shape[0] // OUT_PARTS
    got_x = []
    for c in range(OUT_PARTS):
        part_x = lax.dot_general(
            grad_pregate, gate_w[c * width : (c + 1) * width], columns_both,
            preferred_element_type=jnp.float32,
        )
        part_x = part_x + lax.dot_general(
            grad_preup, up_w[c * width : (c + 1) * width], columns_both,
            preferred_element_type=jnp.float32,
        )
        got_x.append(collect(part_x.astype(jnp.bfloat16)))
    got_g = collect(part_g.reshape(local_count * node_count, capacity)).reshape(-1)
    rows_first = (((0,), (0,)), ((), ()))
    grad_gate = jnp.concatenate(
        [
            lax.dot_general(
                r, grad_pregate, rows_first, preferred_element_type=jnp.float32
            ).astype(jnp.bfloat16)
            for r in rows_x
        ]
    )
    grad_up = jnp.concatenate(
        [
            lax.dot_general(
                r, grad_preup, rows_first, preferred_element_type=jnp.float32
            ).astype(jnp.bfloat16)
            for r in rows_x
        ]
    )
    grad_down = jnp.concatenate(
        [
            lax.dot_general(
                activated,
                (gate_scale * r.astype(jnp.float32)).astype(jnp.bfloat16),
                rows_first,
                preferred_element_type=jnp.float32,
            ).astype(jnp.bfloat16)
            for r in rows_dy
        ],
        axis=1,
    )
    grad_tokens = jnp.concatenate(
        [
            lax.dot_general(
                token_mask, got, rows_first, preferred_element_type=jnp.float32
            ).astype(jnp.bfloat16)
            for got in got_x
        ],
        axis=1,
    )
    grad_routes = jnp.sum(jnp.where(by_route, got_g[:, None], 0.0), axis=0).reshape(
        tok_count, top_count
    )
    return (
        grad_tokens,
        grad_routes,
        grad_gate.reshape(gate_proj.shape),
        grad_up.reshape(up_proj.shape),
        grad_down.reshape(down_proj.shape),
    )


def solution(mesh):
    token_spec = P(("node", "local"), None)
    wide_spec = P("node", None, "local")
    tall_spec = P("node", "local", None)
    return jax.shard_map(
        shards,
        mesh=mesh,
        in_specs=(token_spec,) * 4 + (wide_spec, wide_spec, tall_spec),
        out_specs=(token_spec, token_spec, wide_spec, wide_spec, tall_spec),
        check_vma=False,
    )
```

time: 850 us -> 447 us (0.53)
  waiting for transfers between devices: 675 us -> 92.5 us
  blocking collectives: 8.85 us -> 173 us
  between operations: 0.76 us -> 15.3 us
  local copies, waits for them, and re-layouts: 15.6 us -> 3.15 us
  other arithmetic: 14.7 us -> 25.2 us
    all_to_all x4 -> x3, waiting for transfers between devices: 675 us -> 13 us  [collect(): return lax.all_to_all(near, 'node', split_axis=0, concat_axis=0, tiled=True)]
    all_to_all x1 -> x5, blocking collectives: 8.85 us -> 157 us  [spread(): near = lax.all_to_all(rows, 'node', split_axis=0, concat_axis=0, tiled=True)]
    reduce_scatter x0 -> x2, waiting for transfers between devices: none -> 55 us  [collect(): near = lax.psum_scatter(rows, 'local', scatter_dimension=0, tiled=True)]
    all_gather x0 -> x4, waiting for transfers between devices: none -> 24.4 us  [spread(): return lax.all_gather(near, 'local', axis=0, tiled=True)]
    reshape x0 -> x2, other arithmetic: none -> 17.4 us  [the longest x1 10.4 us: shards(): grad_gate.reshape(gate_proj.shape)]
    broadcast_in_dim x4 -> x1, local copies, waits for them, and re-layouts: 14.7 us -> 0.08 us  [shards(): jnp.where(by_route, got_g[:, None], 0.0)]
    unnamed x0 -> x1, blocking collectives: none -> 10.2 us
    reduce_sum x3 -> x1, other arithmetic: 9.91 us -> 0.62 us  [shards(): jnp.sum(jnp.where(by_route, got_g[:, None], 0.0), axis=0)]
  transfers between devices with their start and end apart: 4 -> 9, of which waited for: 4 -> 5; matrix products, arithmetic and copies ran while one was open for 8% -> 25% of each run, Pallas kernels for 0% -> 0%
where the time goes in v1:
time: 447 us; the launch traced here: 443 us
  blocking collectives  173 us (39%)
  matrix products  117 us (26%)
  waiting for transfers between devices  92.5 us (21%)
  other arithmetic  25.2 us (6%)
  starting transfers between devices  17.1 us (4%)
  between operations  15.3 us (3%)
    all_to_all x5, blocking collectives, spread(): near = lax.all_to_all(rows, 'node', split_axis=0, concat_axis=0, tiled=True)  157 us
    reduce_scatter x2, waiting for transfers between devices, collect(): near = lax.psum_scatter(rows, 'local', scatter_dimension=0, tiled=True)  55 us
    all_gather x4, waiting for transfers between devices, spread(): return lax.all_gather(near, 'local', axis=0, tiled=True)  24.4 us
    all_to_all x3, starting transfers between devices, collect(): return lax.all_to_all(near, 'node', split_axis=0, concat_axis=0, tiled=True)  16.9 us
    dot_general x2, matrix products, shards(): lax.dot_general(r, columns(down_w, c, IN_PARTS), columns_both, preferred_...  16.5 us
    dot_general x2, matrix products, shards(): lax.dot_general(grad_preup, up_w[c * width:(c + 1) * width], columns_both...  15.3 us
    dot_general x2, matrix products, shards(): lax.dot_general(r, grad_preup, rows_first, preferred_element_type=jnp.flo...  14.8 us
    dot_general x2, matrix products, shards(): jnp.dot(r, gate_w[c * width:(c + 1) * width], preferred_element_type=jnp....  14.6 us
  transfers between devices with their start and end apart: 9, of which 5 were waited for; matrix products, arithmetic and copies ran while one was open for 25% of the time, Pallas kernels for 0%

profile of v1, /device:TPU:0, one launch (start us, length us, event | category | flops | bytes accessed | tf_op | source)
XLA Modules:
  0.0 443.3 jit_solution(8135232405194535164)
XLA Ops:
  10.5 40.6 %all_to_all.90 = bf16[8,24,3584]{2,1,0:T(8,128)(2,1)} all-to-all(bf16[8,24,3584]{2,1,0:T(8,128)(2,1)S(1)} %bitcast.83), channel_id=1, replica_groups=mesh['node'=8,'local'=4] {'node'}, dimensions={0} | all-to-all | bytes 2752512 | tf_op jit(solution)/shard_map/all_to_all | solution.py:41
  53.0 36.1 %all_to_all.91 = bf16[8,24,3584]{2,1,0:T(8,128)(2,1)} all-to-all(bf16[8,24,3584]{2,1,0:T(8,128)(2,1)S(1)} %bitcast.84), channel_id=1, replica_groups=mesh['node'=8,'local'=4] {'node'}, dimensions={0} | all-to-all | bytes 2752512 | tf_op jit(solution)/shard_map/all_to_all | solution.py:41
  89.7 35.9 %all_to_all.92 = bf16[8,24,3584]{2,1,0:T(8,128)(2,1)} all-to-all(bf16[8,24,3584]{2,1,0:T(8,128)(2,1)S(1)} %bitcast.85), channel_id=1, replica_groups=mesh['node'=8,'local'=4] {'node'}, dimensions={0} | all-to-all | bytes 2752512 | tf_op jit(solution)/shard_map/all_to_all | solution.py:41
  126.2 35.8 %all_to_all.93 = bf16[8,24,3584]{2,1,0:T(8,128)(2,1)} all-to-all(bf16[8,24,3584]{2,1,0:T(8,128)(2,1)S(1)} %bitcast.86), channel_id=1, replica_groups=mesh['node'=8,'local'=4] {'node'}, dimensions={0} | all-to-all | bytes 2752512 | tf_op jit(solution)/shard_map/all_to_all | solution.py:41
  163.3 6.9 %fusion.8 = f32[768,512]{0,1:T(8,128)S(1)} fusion(bf16[768,3584]{1,0:T(8,128)(2,1)} %all-gather.12.cloned.1.call-done, bf16[1,7168,512]{2,1,0:T(8,128)(2,1)} %param.11), kind=kOutput, calls=%fused_computation.27 | convolution fusion | flops 2818572288 | bytes 10747904 | tf_op jit(solution)/shard_map/dot_general | solution.py:66
  176.5 7.9 %fusion.2 = f32[768,512]{0,1:T(8,128)} fusion(bf16[768,3584]{1,0:T(8,128)(2,1)} %all-gather.8.cloned.1.call-done, bf16[512,7168]{1,0:T(8,128)(2,1)} %bitcast.90), kind=kOutput, calls=%fused_computation.21 | convolution fusion | flops 2818572288 | bytes 10747904 | tf_op jit(solution)/shard_map/dot_general | solution.py:78
  184.4 7.7 %fusion.32 = f32[768,512]{0,1:T(8,128)S(1)} fusion(f32[768,512]{0,1:T(8,128)S(1)} %fusion.8, bf16[768,3584]{1,0:T(8,128)(2,1)} %all-gather.10.cloned.1.call-done, bf16[1,7168,512]{2,1,0:T(8,128)(2,1)} %param.11), kind=kOutput, calls=%fused_computation.55 | convolution fusion | flops 2818965504 | bytes 12320768 | tf_op jit(solution)/shard_map/dot_general | solution.py:66
  197.5 24.4 %all-gather.6.cloned.1.call-done = bf16[768,3584]{1,0:T(8,128)(2,1)} async-done(((bf16[192,3584]{1,0:T(8,128)(2,1)}), bf16[768,3584]{1,0:T(8,128)(2,1)}) %all-gather.6.cloned.1.call-update) | async-done | bytes 5505040 | tf_op jit(solution)/shard_map/all_gather | solution.py:42
  222.0 8.6 %multiply_reduce_fusion = (f32[768]{0:T(1024)S(1)}, bf16[768,512]{0,1:T(8,128)(2,1)}, f32[768,512]{0,1:T(8,128)}) fusion(f32[768,512]{0,1:T(8,128)S(1)} %fusion.29, f32[768,512]{0,1:T(8,128)S(1)} %fusion.32, f32[768,512]{0,1:T(8,128)} %fusion.2, bf16[768,3584]{1,0:T(8,128)(2,1)} %all-gather.6.cloned.1.call-done, bf16[512,7168]{1,0:T(8,128)(2,1)} %bitcast.91), kind=kOutput, calls=%fused_computation.48 | convolution fusion | flops 2822503680 | bytes 16256000 | tf_op jit(solution)/shard_map/dot_general | solution.py:78
  230.7 10.2 %all-reduce = f32[32,24]{1,0:T(8,128)S(1)} all-reduce(f32[32,24]{1,0:T(8,128)S(1)} %reshape.94), channel_id=5, replica_groups=mesh['node'=8,'local'=4] {'local'}, use_global_device_ids=true, to_apply=%region_5.6.clone | all-reduce | flops 768 | bytes 6144
  247.2 6.3 %all-to-all-done.7 = f32[8,1,24]{2,1,0:T(1,128)S(1)} async-done(((f32[8,1,24]{2,1,0:T(1,128)}), f32[8,1,24]{2,1,0:T(1,128)S(1)}, u32[]{:S(2)}, u32[]{:S(2)}) %all-to-all-start.7) | async-done | bytes 800 | tf_op jit(solution)/shard_map/all_to_all | solution.py:46
  255.5 8.8 %all_to_all.94 = bf16[8,1,24]{2,1,0:T(2,128)(2,1)S(1)} all-to-all(bf16[8,1,24]{2,1,0:T(2,128)(2,1)S(1)} %convert_element_type.137), channel_id=1, replica_groups=mesh['node'=8,'local'=4] {'node'}, dimensions={0} | all-to-all | bytes 768 | tf_op jit(solution)/shard_map/all_to_all | solution.py:41
  272.0 8.4 %fusion.6 = f32[768,3584]{1,0:T(8,128)} fusion(bf16[768,512]{0,1:T(8,128)(2,1)S(1)} %get-tuple-element.10, bf16[1,7168,512]{2,1,0:T(8,128)(2,1)} %param.11), kind=kOutput, calls=%fused_computation.25 | convolution fusion | flops 2818572288 | bytes 15466496 | tf_op jit(solution)/shard_map/dot_general | solution.py:93
  280.4 7.5 %add_convert_fusion = bf16[768,3584]{1,0:T(8,128)(2,1)} fusion(f32[768,3584]{1,0:T(8,128)} %fusion.6, bf16[768,512]{0,1:T(8,128)(2,1)S(1)} %get-tuple-element.9, bf16[1,7168,512]{2,1,0:T(8,128)(2,1)S(1)} %bitcast.93), kind=kOutput, calls=%fused_computation.2 | convolution fusion | flops 2824077312 | bytes 20971520 | tf_op jit(solution)/shard_map/dot_general | solution.py:97
  294.6 7.8 %add_convert_fusion.1 = bf16[768,3584]{1,0:T(8,128)(2,1)} fusion(f32[768,3584]{1,0:T(8,128)S(1)} %fusion.10, bf16[768,512]{0,1:T(8,128)(2,1)S(1)} %copy-done.5, bf16[1,7168,512]{2,1,0:T(8,128)(2,1)} %param.12), kind=kOutput, calls=%fused_computation.3 | convolution fusion | flops 2824077312 | bytes 20971520 | tf_op jit(solution)/shard_map/dot_general | solution.py:97
  302.5 7.2 %convolution_convert_fusion.2 = bf16[3584,512]{1,0:T(8,128)(2,1)} fusion(bf16[768,3584]{1,0:T(8,128)(2,1)} %all-gather.12.cloned.1.call-done, bf16[768,512]{0,1:T(8,128)(2,1)S(1)} %copy-done.5), kind=kOutput, calls=%fused_computation.9 | convolution fusion | flops 2820407296 | bytes 9961472 | tf_op jit(solution)/shard_map/dot_general | solution.py:114
  309.7 28.8 %reduce-scatter.5.cloned.1.call-done = bf16[192,3584]{1,0:T(8,128)(2,1)} async-done(((bf16[768,3584]{1,0:T(8,128)(2,1)}), bf16[192,3584]{1,0:T(8,128)(2,1)}) %reduce-scatter.5.cloned.1.call-update) | async-done | bytes 1376272 | tf_op jit(solution)/shard_map/reduce_scatter | solution.py:45
  344.0 7.4 %convolution_convert_fusion.4 = bf16[3584,512]{1,0:T(8,128)(2,1)} fusion(bf16[768,3584]{1,0:T(8,128)(2,1)} %all-gather.12.cloned.1.call-done, bf16[768,512]{0,1:T(8,128)(2,1)S(1)} %copy-done.3), kind=kOutput, calls=%fused_computation.11 | convolution fusion | flops 2820407296 | bytes 9961472 | tf_op jit(solution)/shard_map/dot_general | solution.py:106
  351.4 7.6 %convolution_convert_fusion.3 = bf16[3584,512]{1,0:T(8,128)(2,1)} fusion(bf16[768,3584]{1,0:T(8,128)(2,1)} %all-gather.10.cloned.1.call-done, bf16[768,512]{0,1:T(8,128)(2,1)S(1)} %copy-done.5), kind=kOutput, calls=%fused_computation.10 | convolution fusion | flops 2820407296 | bytes 9961472 | tf_op jit(solution)/shard_map/dot_general | solution.py:114
  368.6 26.1 %reduce-scatter.3.cloned.1.call-done = bf16[192,3584]{1,0:T(8,128)(2,1)} async-done(((bf16[768,3584]{1,0:T(8,128)(2,1)}), bf16[192,3584]{1,0:T(8,128)(2,1)}) %reduce-scatter.3.cloned.1.call-update) | async-done | bytes 1376272 | tf_op jit(solution)/shard_map/reduce_scatter | solution.py:45
  400.5 7.2 %convolution_convert_fusion.5 = bf16[3584,512]{1,0:T(8,128)(2,1)} fusion(bf16[768,3584]{1,0:T(8,128)(2,1)} %all-gather.10.cloned.1.call-done, bf16[768,512]{0,1:T(8,128)(2,1)S(1)} %copy-done.3), kind=kOutput, calls=%fused_computation.12 | convolution fusion | flops 2820407296 | bytes 9961472 | tf_op jit(solution)/shard_map/dot_general | solution.py:106
  407.7 7.0 %maximum_bitcast_fusion.2 = bf16[1,512,7168]{2,1,0:T(8,128)(2,1)} fusion(bf16[512,3584]{1,0:T(8,128)(2,1)} %convolution_convert_fusion, bf16[512,3584]{1,0:T(8,128)(2,1)} %convolution_convert_fusion.1), kind=kLoop, calls=%fused_computation.6 | loop fusion | flops 14680064 | bytes 14680064 | tf_op jit(solution)/shard_map/reshape | solution.py:149
  414.7 10.4 %maximum_bitcast_fusion = (bf16[1,7168,512]{2,1,0:T(8,128)(2,1)}, bf16[1,7168,512]{2,1,0:T(8,128)(2,1)}) fusion(bf16[3584,512]{1,0:T(8,128)(2,1)} %convolution_convert_fusion.4, bf16[3584,512]{1,0:T(8,128)(2,1)} %convolution_convert_fusion.5, bf16[3584,512]{1,0:T(8,128)(2,1)} %convolution_convert_fusion.2, bf16[3584,512]{1,0:T(8,128)(2,1)} %convolution_convert_fusion.3), kind=kLoop, calls=%fused_computation.4 | loop fusion | flops 29360128 | bytes 29360128 | tf_op jit(solution)/shard_map/reshape | solution.py:147
  426.5 6.7 %all-to-all-done.5 = bf16[8,24,3584]{2,1,0:T(8,128)(2,1)S(1)} async-done(((bf16[8,24,3584]{2,1,0:T(8,128)(2,1)}), bf16[8,24,3584]{2,1,0:T(8,128)(2,1)S(1)}, u32[]{:S(2)}, u32[]{:S(2)}) %all-to-all-start.5) | async-done | bytes 1376288 | tf_op jit(solution)/shard_map/all_to_all | solution.py:46
  (85 shorter events, 66.4 us)
Async XLA Ops:
  7.2 156.1 %all-gather.12.cloned.1.call-start = ((), (), s32[]{:S(2)}) async-start(), calls=%async_computation.13 | async-start | bytes 6881280 | tf_op jit(solution)/shard_map/all_gather | solution.py:42
  51.1 38.1 %copy-start = (bf16[128,7168]{1,0:T(8,128)(2,1)S(1)}, bf16[128,7168]{1,0:T(8,128)(2,1)}, u32[]{:S(2)}) copy-start(bf16[128,7168]{1,0:T(8,128)(2,1)} %param.7) | copy-start | bytes 5505028
  51.1 125.4 %all-gather.8.cloned.1.call-start = ((), (), s32[]{:S(2)}) async-start(), calls=%async_computation.11 | async-start | bytes 6881280 | tf_op jit(solution)/shard_map/all_gather | solution.py:42
  89.1 95.3 %all-gather.10.cloned.1.call-start = ((), (), s32[]{:S(2)}) async-start(), calls=%async_computation.12 | async-start | bytes 6881280 | tf_op jit(solution)/shard_map/all_gather | solution.py:42
  89.7 36.0 %copy-start.1 = (bf16[128,7168]{1,0:T(8,128)(2,1)S(1)}, bf16[128,7168]{1,0:T(8,128)(2,1)}, u32[]{:S(2)}) copy-start(bf16[128,7168]{1,0:T(8,128)(2,1)} %param.8) | copy-start | bytes 5505028
  125.6 36.4 %copy-start.9 = (u32[32]{0:T(128)S(1)}, u32[32]{0:T(128)}, u32[]{:S(2)}) copy-start(u32[32]{0:T(128)} %constant.14) | copy-start | bytes 388
  125.6 96.3 %all-gather.6.cloned.1.call-start = ((), (), s32[]{:S(2)}) async-start(), calls=%async_computation.10 | async-start | bytes 6881280 | tf_op jit(solution)/shard_map/all_gather | solution.py:42
  184.4 7.8 %copy-start.7 = (bf16[768,3584]{1,0:T(8,128)(2,1)S(1)}, bf16[768,3584]{1,0:T(8,128)(2,1)}, u32[]{:S(2)}) copy-start(bf16[768,3584]{1,0:T(8,128)(2,1)} %all-gather.10.cloned.1.call-done) | copy-start | bytes 16515076
  184.4 7.8 %copy-start.10 = (f32[768,512]{0,1:T(8,128)S(1)}, f32[768,512]{0,1:T(8,128)}, u32[]{:S(2)}) copy-start(f32[768,512]{0,1:T(8,128)} %fusion.15) | copy-start | bytes 4718596
  197.5 49.7 %copy-start.8 = (bf16[128,1]{0,1:T(2,128)(2,1)S(1)}, bf16[128,1]{0,1:T(2,128)(2,1)}, u32[]{:S(2)}) copy-start(bf16[128,1]{0,1:T(2,128)(2,1)} %param.10) | copy-start | bytes 772
  241.5 12.1 %all-to-all-start.7 = ((f32[8,1,24]{2,1,0:T(1,128)}), f32[8,1,24]{2,1,0:T(1,128)S(1)}, u32[]{:S(2)}, u32[]{:S(2)}) async-start(f32[8,1,24]{2,1,0:T(1,128)} %bitcast.20), calls=%async_computation.9 | async-start | bytes 8192 | tf_op jit(solution)/shard_map/all_to_all | solution.py:46
  247.2 91.3 %reduce-scatter.5.cloned.1.call-start = ((), (), s32[]{:S(2)}) async-start(), calls=%async_computation.15 | async-start | bytes 6881280 | tf_op jit(solution)/shard_map/reduce_scatter | solution.py:45
  269.6 10.8 %slice-start = ((s8[7340032]{0:T(1024)(128)(4,1)}), s8[4194304]{0:T(1024)(128)(4,1)S(1)}, s32[]{:S(2)}) async-start(s8[7340032]{0:T(1024)(128)(4,1)} %bitcast.92), calls=%async_computation.16 | async-start | bytes 8388608
  271.9 8.5 %copy-start.2 = (bf16[768,512]{0,1:T(8,128)(2,1)}, bf16[768,512]{0,1:T(8,128)(2,1)S(1)}, u32[]{:S(2)}) copy-start(bf16[768,512]{0,1:T(8,128)(2,1)S(1)} %get-tuple-element.10) | copy-start | bytes 2359300
  271.9 8.4 %copy-start.4 = (bf16[768,512]{0,1:T(8,128)(2,1)}, bf16[768,512]{0,1:T(8,128)(2,1)S(1)}, u32[]{:S(2)}) copy-start(bf16[768,512]{0,1:T(8,128)(2,1)S(1)} %get-tuple-element.9) | copy-start | bytes 2359300
  272.0 8.4 %slice-start.1 = ((s8[7340032]{0:T(1024)(128)(4,1)}), s8[3145728]{0:T(1024)(128)(4,1)S(1)}, s32[]{:S(2)}) async-start(s8[7340032]{0:T(1024)(128)(4,1)} %bitcast.92), calls=%async_computation.17 | async-start | bytes 6291456
  288.0 106.8 %reduce-scatter.3.cloned.1.call-start = ((), (), s32[]{:S(2)}) async-start(), calls=%async_computation.14 | async-start | bytes 6881280 | tf_op jit(solution)/shard_map/reduce_scatter | solution.py:45
  338.5 56.3 %all-to-all-start.6 = ((bf16[8,24,3584]{2,1,0:T(8,128)(2,1)}), bf16[8,24,3584]{2,1,0:T(8,128)(2,1)S(1)}, u32[]{:S(2)}, u32[]{:S(2)}) async-start(bf16[8,24,3584]{2,1,0:T(8,128)(2,1)} %bitcast.88), calls=%async_computation.8 | async-start | bytes 2752512 | tf_op jit(solution)/shard_map/all_to_all | solution.py:46
  344.0 15.0 %slice-start.2 = ((s8[5505024]{0:T(1024)(128)(4,1)}), s8[4194304]{0:T(1024)(128)(4,1)S(1)}, s32[]{:S(2)}) async-start(s8[5505024]{0:T(1024)(128)(4,1)} %bitcast.94), calls=%async_computation.18 | async-start | bytes 8388608
  344.0 19.8 %slice-start.4 = ((s8[5505024]{0:T(1024)(128)(4,1)}), s8[4194304]{0:T(1024)(128)(4,1)S(1)}, s32[]{:S(2)}) async-start(s8[5505024]{0:T(1024)(128)(4,1)} %bitcast.96), calls=%async_computation.20 | async-start | bytes 8388608
  351.4 7.7 %slice-start.3 = ((s8[5505024]{0:T(1024)(128)(4,1)}), s8[1310720]{0:T(1024)(128)(4,1)S(1)}, s32[]{:S(2)}) async-start(s8[5505024]{0:T(1024)(128)(4,1)} %bitcast.94), calls=%async_computation.19 | async-start | bytes 2621440
  351.4 7.7 %copy-start.11 = (bf16[768,512]{0,1:T(8,128)(2,1)S(1)}, bf16[768,512]{0,1:T(8,128)(2,1)}, u32[]{:S(2)}) copy-start(bf16[768,512]{0,1:T(8,128)(2,1)} %get-tuple-element.8) | copy-start | bytes 2359300
  351.4 12.4 %slice-start.5 = ((s8[5505024]{0:T(1024)(128)(4,1)}), s8[1310720]{0:T(1024)(128)(4,1)S(1)}, s32[]{:S(2)}) async-start(s8[5505024]{0:T(1024)(128)(4,1)} %bitcast.96), calls=%async_computation.21 | async-start | bytes 2621440
  394.8 38.5 %all-to-all-start.5 = ((bf16[8,24,3584]{2,1,0:T(8,128)(2,1)}), bf16[8,24,3584]{2,1,0:T(8,128)(2,1)S(1)}, u32[]{:S(2)}, u32[]{:S(2)}) async-start(bf16[8,24,3584]{2,1,0:T(8,128)(2,1)} %bitcast.87), calls=%async_computation.6 | async-start | bytes 2752512 | tf_op jit(solution)/shard_map/all_to_all | solution.py:46
  (3 other events, 14.7 us)
Sparse Core Ops, SparseCore 0:
  51.2 40.2 all-gather.11
  93.1 41.9 all-gather.7
  136.6 41.9 all-gather.9
  180.0 41.9 all-gather.5
  288.1 50.3 reduce-scatter.4
  341.6 53.0 reduce-scatter.2

commit v2 on v1

--- a/solution.py
+++ b/solution.py
@@ -3,8 +3,10 @@
 from jax import lax
 from jax.sharding import PartitionSpec as P
 
-IN_PARTS = 2
-OUT_PARTS = 2
+X_CUTS = (0, 2, 4)
+DY_CUTS = (0, 2, 3, 4)
+OUT_PARTS = 4
+LANES = 128
 
 
 def slot_tables(route_ids, experts, capacity):
@@ -22,11 +24,6 @@
     return (by_route, by_token)
 
 
-def columns(array, part, parts):
-    width = array.shape[1] // parts
-    return array[:, part * width : (part + 1) * width]
-
-
 def shards(tokens, out_grad, route_ids, route_weights, gate_proj, up_proj, down_proj):
     node_count = lax.axis_size("node")
     local_count = lax.axis_size("local")
@@ -36,39 +33,50 @@
     token_mask = by_token.astype(jnp.bfloat16)
     weight_line = route_weights.reshape(1, tok_count * top_count).astype(jnp.float32)
     send_g = jnp.sum(jnp.where(by_route, weight_line, 0.0), axis=1).astype(jnp.bfloat16)
+    send_g = jnp.broadcast_to(send_g[:, None], (node_count * capacity, LANES))
+
+    def swap(rows, bit):
+        pairs = [(i, i ^ bit) for i in range(local_count)]
+        return lax.ppermute(rows, "local", pairs)
 
     def spread(rows):
-        near = lax.all_to_all(rows, "node", split_axis=0, concat_axis=0, tiled=True)
-        return lax.all_gather(near, "local", axis=0, tiled=True)
+        rows = lax.all_to_all(rows, "node", split_axis=0, concat_axis=0, tiled=True)
+        bit = 2
+        while bit < local_count:
+            rows = jnp.concatenate([rows, swap(rows, bit)])
+            bit = 2 * bit
+        return jnp.concatenate([rows, swap(rows, 1)])
 
     def collect(rows):
-        near = lax.psum_scatter(rows, "local", scatter_dimension=0, tiled=True)
-        return lax.all_to_all(near, "node", split_axis=0, concat_axis=0, tiled=True)
+        for bit in [1] + [local_count >> k for k in range(1, local_count.bit_length() - 1)]:
+            keep, give = jnp.split(rows, 2)
+            got = swap(give, bit)
+            rows = (keep.astype(jnp.float32) + got.astype(jnp.float32)).astype(jnp.bfloat16)
+        return lax.all_to_all(rows, "node", split_axis=0, concat_axis=0, tiled=True)
 
-    def dispatch(array):
-        return [
-            spread(
-                jnp.dot(
-                    token_mask, columns(array, c, IN_PARTS), preferred_element_type=jnp.float32
-                ).astype(jnp.bfloat16)
-            )
-            for c in range(IN_PARTS)
-        ]
+    unit = tokens.shape[1] // X_CUTS[-1]
+    x_spans = [(a * unit, b * unit) for a, b in zip(X_CUTS, X_CUTS[1:])]
+    dy_spans = [(a * unit, b * unit) for a, b in zip(DY_CUTS, DY_CUTS[1:])]
 
-    rows_x = dispatch(tokens)
-    rows_g = spread(send_g.reshape(node_count, capacity)).reshape(-1)
-    rows_dy = dispatch(out_grad)
+    def pick(array, span):
+        part = array[:, span[0] : span[1]]
+        rows = jnp.dot(token_mask, part, preferred_element_type=jnp.float32)
+        return rows.astype(jnp.bfloat16)
+
+    first_rows = spread(jnp.concatenate([pick(tokens, x_spans[0]), send_g], axis=1))
+    rows_g = first_rows[:, -1]
+    rows_x = [first_rows[:, :-LANES]] + [spread(pick(tokens, span)) for span in x_spans[1:]]
+    rows_dy = [spread(pick(out_grad, span)) for span in dy_spans]
     gate_w = gate_proj[0]
     up_w = up_proj[0]
     down_w = down_proj[0]
-    width = gate_w.shape[0] // IN_PARTS
     pre_gate = sum(
-        jnp.dot(r, gate_w[c * width : (c + 1) * width], preferred_element_type=jnp.float32)
-        for c, r in enumerate(rows_x)
+        jnp.dot(r, gate_w[a:b], preferred_element_type=jnp.float32)
+        for (a, b), r in zip(x_spans, rows_x)
     )
     pre_up = sum(
-        jnp.dot(r, up_w[c * width : (c + 1) * width], preferred_element_type=jnp.float32)
-        for c, r in enumerate(rows_x)
+        jnp.dot(r, up_w[a:b], preferred_element_type=jnp.float32)
+        for (a, b), r in zip(x_spans, rows_x)
     )
     gate_sigmoid = jax.nn.sigmoid(pre_gate)
     gate_silu = pre_gate * gate_sigmoid
@@ -76,9 +84,9 @@
     columns_both = (((1,), (1,)), ((), ()))
     back_proj = sum(
         lax.dot_general(
-            r, columns(down_w, c, IN_PARTS), columns_both, preferred_element_type=jnp.float32
+            r, down_w[:, a:b], columns_both, preferred_element_type=jnp.float32
         )
-        for c, r in enumerate(rows_dy)
+        for (a, b), r in zip(dy_spans, rows_dy)
     )
     gate_scale = rows_g.astype(jnp.float32)[:, None]
     grad_act = gate_scale * back_proj
@@ -98,8 +106,13 @@
             grad_preup, up_w[c * width : (c + 1) * width], columns_both,
             preferred_element_type=jnp.float32,
         )
-        got_x.append(collect(part_x.astype(jnp.bfloat16)))
-    got_g = collect(part_g.reshape(local_count * node_count, capacity)).reshape(-1)
+        part_x = part_x.astype(jnp.bfloat16)
+        if c == OUT_PARTS - 1:
+            lanes_g = jnp.broadcast_to(part_g.astype(jnp.bfloat16)[:, None], (part_g.shape[0], LANES))
+            part_x = jnp.concatenate([part_x, lanes_g], axis=1)
+        got_x.append(collect(part_x))
+    got_g = got_x[-1][:, -1].astype(jnp.float32)
+    got_x[-1] = got_x[-1][:, :-LANES]
     rows_first = (((0,), (0,)), ((), ()))
     grad_gate = jnp.concatenate(
         [

time: 447 us -> 478 us (1.069)
  blocking collectives: 173 us -> 0 us
  waiting for transfers between devices: 92.5 us -> 228 us
  starting transfers between devices: 17.1 us -> 52.5 us
  other arithmetic: 25.2 us -> 48.5 us
  between operations: 15.3 us -> 1.36 us
  local copies, waits for them, and re-layouts: 3.15 us -> 15.7 us
  matrix products: 117 us -> 128 us
    all_to_all x5 -> x0, blocking collectives: 157 us -> none  [spread(): near = lax.all_to_all(rows, 'node', split_axis=0, concat_axis=0, tiled=True)]
    ppermute x0 -> x18, waiting for transfers between devices: none -> 113 us  [swap(): return lax.ppermute(rows, 'local', pairs)]
    all_to_all x3 -> x9, waiting for transfers between devices: 13 us -> 114 us  [the longest x5 92.4 us: spread(): rows = lax.all_to_all(rows, 'node', split_axis=0, concat_axis=0, tiled=True)]
    reduce_scatter x2 -> x0, waiting for transfers between devices: 55 us -> none  [collect(): near = lax.psum_scatter(rows, 'local', scatter_dimension=0, tiled=True)]
    all_gather x4 -> x0, waiting for transfers between devices: 24.4 us -> none  [spread(): return lax.all_gather(near, 'local', axis=0, tiled=True)]
    all_to_all x3 -> x9, starting transfers between devices: 16.9 us -> 39.8 us  [the longest x5 22.3 us: spread(): rows = lax.all_to_all(rows, 'node', split_axis=0, concat_axis=0, tiled=True)]
    convert_element_type x1 -> x8, other arithmetic: 2.33 us -> 15.2 us  [collect(): (keep.astype(jnp.float32) + got.astype(jnp.float32)).astype(jnp.bfloat16)]
    ppermute x0 -> x18, starting transfers between devices: none -> 12.7 us  [swap(): return lax.ppermute(rows, 'local', pairs)]
  transfers between devices with their start and end apart: 9 -> 27, of which waited for: 5 -> 13; matrix products, arithmetic and copies ran while one was open for 25% -> 32% of each run, Pallas kernels for 0% -> 0%
where the time goes in v2:
time: 478 us; the launch traced here: 474 us
  waiting for transfers between devices  228 us (48%)
  matrix products  128 us (27%)
  starting transfers between devices  52.5 us (11%)
  other arithmetic  48.5 us (10%)
  local copies, waits for them, and re-layouts  15.7 us (3%)
    ppermute x18, waiting for transfers between devices, swap(): return lax.ppermute(rows, 'local', pairs)  113 us
    all_to_all x5, waiting for transfers between devices, spread(): rows = lax.all_to_all(rows, 'node', split_axis=0, concat_axis=0, tiled=True)  92.4 us
    all_to_all x5, starting transfers between devices, spread(): rows = lax.all_to_all(rows, 'node', split_axis=0, concat_axis=0, tiled=True)  22.3 us
    all_to_all x4, waiting for transfers between devices, collect(): return lax.all_to_all(rows, 'node', split_axis=0, concat_axis=0, tiled=True)  21.8 us
    all_to_all x4, starting transfers between devices, collect(): return lax.all_to_all(rows, 'node', split_axis=0, concat_axis=0, tiled=True)  17.5 us
    dot_general x2, matrix products, shards(): lax.dot_general(r, grad_preup, rows_first, preferred_element_type=jnp.flo...  17.4 us
    dot_general x3, matrix products, shards(): lax.dot_general(r, down_w[:, a:b], columns_both, preferred_element_type=j...  16.8 us
    dot_general x3, matrix products, shards(): lax.dot_general(activated, (gate_scale * r.astype(jnp.float32)).astype(jn...  16.8 us
  transfers between devices with their start and end apart: 27, of which 13 were waited for; matrix products, arithmetic and copies ran while one was open for 32% of the time, Pallas kernels for 0%

profile of v2, /device:TPU:0, one launch (start us, length us, event | category | flops | bytes accessed | tf_op | source)
XLA Modules:
  0.0 473.9 jit_solution(15202108527970666498)
XLA Ops:
  4.5 7.3 %all-to-all-start.3 = ((bf16[8,24,1792]{2,1,0:T(8,128)(2,1)}), bf16[8,24,1792]{2,1,0:T(8,128)(2,1)S(1)}, u32[]{:S(2)}, u32[]{:S(2)}) async-start(bf16[8,24,1792]{2,1,0:T(8,128)(2,1)} %bitcast.9), calls=%async_computation.3 | async-start | bytes 1376256 | tf_op jit(solution)/shard_map/all_to_all | solution.py:43
  14.0 15.8 %all-to-all-done.3 = bf16[8,24,1792]{2,1,0:T(8,128)(2,1)S(1)} async-done(((bf16[8,24,1792]{2,1,0:T(8,128)(2,1)}), bf16[8,24,1792]{2,1,0:T(8,128)(2,1)S(1)}, u32[]{:S(2)}, u32[]{:S(2)}) %all-to-all-start.3) | async-done | bytes 688160 | tf_op jit(solution)/shard_map/all_to_all | solution.py:43
  35.0 16.6 %all-to-all-done.2 = bf16[8,24,1792]{2,1,0:T(8,128)(2,1)S(1)} async-done(((bf16[8,24,1792]{2,1,0:T(8,128)(2,1)}), bf16[8,24,1792]{2,1,0:T(8,128)(2,1)S(1)}, u32[]{:S(2)}, u32[]{:S(2)}) %all-to-all-start.2) | async-done | bytes 688160 | tf_op jit(solution)/shard_map/all_to_all | solution.py:43
  58.0 30.2 %all-to-all-done.4 = bf16[8,24,3584]{2,1,0:T(8,128)(2,1)S(1)} async-done(((bf16[8,24,3584]{2,1,0:T(8,128)(2,1)}), bf16[8,24,3584]{2,1,0:T(8,128)(2,1)S(1)}, u32[]{:S(2)}, u32[]{:S(2)}) %all-to-all-start.4) | async-done | bytes 1376288 | tf_op jit(solution)/shard_map/all_to_all | solution.py:43
  95.0 29.9 %all-to-all-done.1 = bf16[8,24,3584]{2,1,0:T(8,128)(2,1)S(1)} async-done(((bf16[8,24,3584]{2,1,0:T(8,128)(2,1)}), bf16[8,24,3584]{2,1,0:T(8,128)(2,1)S(1)}, u32[]{:S(2)}, u32[]{:S(2)}) %all-to-all-start.1) | async-done | bytes 1376288 | tf_op jit(solution)/shard_map/all_to_all | solution.py:43
  133.6 29.6 %collective-permute-done.8 = bf16[192,3584]{1,0:T(8,128)(2,1)S(1)} collective-permute-done((bf16[192,3584]{1,0:T(8,128)(2,1)S(1)}, bf16[192,3584]{1,0:T(8,128)(2,1)S(1)}, u32[]{:S(2)}, u32[]{:S(2)}) %collective-permute-start.8) | collective-permute-done | bytes 1376288 | tf_op jit(solution)/shard_map/ppermute | solution.py:40
  167.4 10.7 %collective-permute-done.4 = bf16[192,1792]{1,0:T(8,128)(2,1)} collective-permute-done((bf16[192,1792]{1,0:T(8,128)(2,1)}, bf16[192,1792]{1,0:T(8,128)(2,1)}, u32[]{:S(2)}, u32[]{:S(2)}) %collective-permute-start.4) | collective-permute-done | bytes 688160 | tf_op jit(solution)/shard_map/ppermute | solution.py:40
  179.5 42.8 %collective-permute-done.6 = bf16[192,1792]{1,0:T(8,128)(2,1)} collective-permute-done((bf16[192,1792]{1,0:T(8,128)(2,1)S(1)}, bf16[192,1792]{1,0:T(8,128)(2,1)}, u32[]{:S(2)}, u32[]{:S(2)}) %collective-permute-start.6) | collective-permute-done | bytes 688160 | tf_op jit(solution)/shard_map/ppermute | solution.py:40
  226.7 24.8 %collective-permute-done = bf16[192,3712]{1,0:T(8,128)(2,1)S(1)} collective-permute-done((bf16[192,3712]{1,0:T(8,128)(2,1)S(1)}, bf16[192,3712]{1,0:T(8,128)(2,1)S(1)}, u32[]{:S(2)}, u32[]{:S(2)}) %collective-permute-start) | collective-permute-done | bytes 1425440 | tf_op jit(solution)/shard_map/ppermute | solution.py:40
  257.6 7.6 %fusion.3 = f32[768,512]{0,1:T(8,128)} fusion(bf16[1,7168,512]{2,1,0:T(8,128)(2,1)} %param.11, bf16[384,3584]{1,0:T(8,128)(2,1)} %collective-permute-done.9, bf16[192,3584]{1,0:T(8,128)(2,1)} %copy-done.28, bf16[192,3584]{1,0:T(8,128)(2,1)S(1)} %bitcast.100), kind=kOutput, calls=%fused_computation.25 | convolution fusion | flops 2835087360 | bytes 10747904 | tf_op jit(solution)/shard_map/dot_general | solution.py:74
  265.3 6.1 %fusion.7 = f32[768,512]{0,1:T(8,128)} fusion(bf16[1,7168,512]{2,1,0:T(8,128)(2,1)S(1)} %bitcast.97, bf16[384,3584]{1,0:T(8,128)(2,1)} %collective-permute-done.9, bf16[192,3584]{1,0:T(8,128)(2,1)S(1)} %copy-done.29, bf16[192,3584]{1,0:T(8,128)(2,1)S(1)} %bitcast.101), kind=kOutput, calls=%fused_computation.29 | convolution fusion | flops 2835087360 | bytes 10747904 | tf_op jit(solution)/shard_map/dot_general | solution.py:78
  271.4 6.3 %fusion.1 = f32[768,512]{0,1:T(8,128)S(1)} fusion(bf16[512,7168]{1,0:T(8,128)(2,1)} %bitcast.124, bf16[384,3584]{1,0:T(8,128)(2,1)} %collective-permute-done.3, bf16[192,3584]{1,0:T(8,128)(2,1)} %collective-permute-done.2, bf16[192,3584]{1,0:T(8,128)(2,1)S(1)} %bitcast.106), kind=kOutput, calls=%fused_computation.23 | convolution fusion | flops 2835087360 | bytes 10747904 | tf_op jit(solution)/shard_map/dot_general | solution.py:86
  284.0 6.9 %fusion.46 = f32[768,512]{0,1:T(8,128)} fusion(f32[768,512]{0,1:T(8,128)} %fusion.3, bf16[1,7168,512]{2,1,0:T(8,128)(2,1)} %param.11, bf16[384,3712]{1,0:T(8,128)(2,1)S(1)} %collective-permute-done.1, bf16[192,3712]{1,0:T(8,128)(2,1)S(1)} %collective-permute-done, bf16[192,3712]{1,0:T(8,128)(2,1)S(1)} %bitcast.93), kind=kOutput, calls=%fused_computation.95 | convolution fusion | flops 2835480576 | bytes 12517376 | tf_op jit(solution)/shard_map/dot_general | solution.py:74
  328.1 6.9 %convolution_convert_fusion.1 = bf16[3584,512]{1,0:T(8,128)(2,1)} fusion(bf16[768,512]{0,1:T(8,128)(2,1)S(1)} %get-tuple-element.8, bf16[384,3584]{1,0:T(8,128)(2,1)} %collective-permute-done.9, bf16[192,3584]{1,0:T(8,128)(2,1)S(1)} %copy-done.30, bf16[192,3584]{1,0:T(8,128)(2,1)S(1)} %bitcast.102), kind=kOutput, calls=%fused_computation.5 | convolution fusion | flops 2836922368 | bytes 9961472 | tf_op jit(solution)/shard_map/dot_general | solution.py:127
  335.0 7.8 %convolution_convert_fusion = bf16[512,3584]{1,0:T(8,128)(2,1)} fusion(bf16[768,512]{0,1:T(8,128)(2,1)S(1)} %copy-done.38, f32[768]{0:T(1024)S(1)} %convert_reduce_fusion, bf16[384,3584]{1,0:T(8,128)(2,1)} %collective-permute-done.3, bf16[192,3584]{1,0:T(8,128)(2,1)} %collective-permute-done.2, bf16[192,3584]{1,0:T(8,128)(2,1)S(1)} %bitcast.107), kind=kOutput, calls=%fused_computation.4 | convolution fusion | flops 2842427392 | bytes 9964544 | tf_op jit(solution)/shard_map/dot_general | solution.py:135
  342.7 10.5 %convolution_convert_fusion.2 = bf16[3584,512]{1,0:T(8,128)(2,1)} fusion(bf16[768,512]{0,1:T(8,128)(2,1)S(1)} %get-tuple-element.8, bf16[384,3712]{1,0:T(8,128)(2,1)S(1)} %copy-done.20, bf16[192,3712]{1,0:T(8,128)(2,1)S(1)} %collective-permute-done, bf16[192,3712]{1,0:T(8,128)(2,1)S(1)} %bitcast.95), kind=kOutput, calls=%fused_computation.6 | convolution fusion | flops 2836922368 | bytes 10158080 | tf_op jit(solution)/shard_map/dot_general | solution.py:127
  353.3 6.7 %maximum_bitcast_fusion.1 = bf16[1,7168,512]{2,1,0:T(8,128)(2,1)} fusion(bf16[3584,512]{1,0:T(8,128)(2,1)} %convolution_convert_fusion.1, bf16[3584,512]{1,0:T(8,128)(2,1)} %convolution_convert_fusion.2), kind=kLoop, calls=%fused_computation.2 | loop fusion | flops 14680064 | bytes 14680064 | tf_op jit(solution)/shard_map/reshape | solution.py:161
  363.8 6.7 %convolution_convert_fusion.3 = bf16[3584,512]{1,0:T(8,128)(2,1)} fusion(bf16[768,512]{0,1:T(8,128)(2,1)S(1)} %copy-done.37, bf16[384,3584]{1,0:T(8,128)(2,1)} %collective-permute-done.9, bf16[192,3584]{1,0:T(8,128)(2,1)S(1)} %copy-done.31, bf16[192,3584]{1,0:T(8,128)(2,1)S(1)} %bitcast.103), kind=kOutput, calls=%fused_computation.7 | convolution fusion | flops 2836922368 | bytes 9961472 | tf_op jit(solution)/shard_map/dot_general | solution.py:119
  381.5 6.0 %all-to-all-start.7 = ((bf16[8,24,1792]{2,1,0:T(8,128)(2,1)}), bf16[8,24,1792]{2,1,0:T(8,128)(2,1)}, u32[]{:S(2)}, u32[]{:S(2)}) async-start(bf16[8,24,1792]{2,1,0:T(8,128)(2,1)} %bitcast.121), calls=%async_computation.7 | async-start | bytes 1376256 | tf_op jit(solution)/shard_map/all_to_all | solution.py:55
  387.5 7.9 %convolution_convert_fusion.4 = bf16[3584,512]{1,0:T(8,128)(2,1)} fusion(bf16[768,512]{0,1:T(8,128)(2,1)} %copy-done.36, bf16[384,3712]{1,0:T(8,128)(2,1)} %copy-done.19, bf16[192,3712]{1,0:T(8,128)(2,1)} %copy-done.9, bf16[192,3712]{1,0:T(8,128)(2,1)} %bitcast.94), kind=kOutput, calls=%fused_computation.8 | convolution fusion | flops 2836922368 | bytes 10158080 | tf_op jit(solution)/shard_map/dot_general | solution.py:119
  409.0 6.7 %maximum_bitcast_fusion = bf16[1,7168,512]{2,1,0:T(8,128)(2,1)} fusion(bf16[3584,512]{1,0:T(8,128)(2,1)} %convolution_convert_fusion.3, bf16[3584,512]{1,0:T(8,128)(2,1)} %convolution_convert_fusion.4), kind=kLoop, calls=%fused_computation.1 | loop fusion | flops 14680064 | bytes 14680064 | tf_op jit(solution)/shard_map/reshape | solution.py:160
  441.5 6.8 %all-to-all-done.5 = bf16[8,24,1792]{2,1,0:T(8,128)(2,1)S(1)} async-done(((bf16[8,24,1792]{2,1,0:T(8,128)(2,1)}), bf16[8,24,1792]{2,1,0:T(8,128)(2,1)S(1)}, u32[]{:S(2)}, u32[]{:S(2)}) %all-to-all-start.5) | async-done | bytes 688160 | tf_op jit(solution)/shard_map/all_to_all | solution.py:55
  451.9 6.0 %maximum_bitcast_fusion.2 = bf16[1,512,7168]{2,1,0:T(8,128)(2,1)} fusion(bf16[512,1792]{1,0:T(8,128)(2,1)} %convolution_convert_fusion.8, bf16[512,1792]{1,0:T(8,128)(2,1)S(1)} %copy-done.24, bf16[512,3584]{1,0:T(8,128)(2,1)} %convolution_convert_fusion), kind=kLoop, calls=%fused_computation.3 | loop fusion | flops 22020096 | bytes 14680064 | tf_op jit(solution)/shard_map/reshape | solution.py:162
  461.1 10.0 %all-to-all-done.8 = bf16[8,24,1920]{2,1,0:T(8,128)(2,1)S(1)} async-done(((bf16[8,24,1920]{2,1,0:T(8,128)(2,1)}), bf16[8,24,1920]{2,1,0:T(8,128)(2,1)S(1)}, u32[]{:S(2)}, u32[]{:S(2)}) %all-to-all-start.8) | async-done | bytes 737312 | tf_op jit(solution)/shard_map/all_to_all | solution.py:55
  (188 shorter events, 156.0 us)
Async XLA Ops:
  4.5 25.3 %all-to-all-start.3 = ((bf16[8,24,1792]{2,1,0:T(8,128)(2,1)}), bf16[8,24,1792]{2,1,0:T(8,128)(2,1)S(1)}, u32[]{:S(2)}, u32[]{:S(2)}) async-start(bf16[8,24,1792]{2,1,0:T(8,128)(2,1)} %bitcast.9), calls=%async_computation.3 | async-start | bytes 1376256 | tf_op jit(solution)/shard_map/all_to_all | solution.py:43
  29.8 21.8 %all-to-all-start.2 = ((bf16[8,24,1792]{2,1,0:T(8,128)(2,1)}), bf16[8,24,1792]{2,1,0:T(8,128)(2,1)S(1)}, u32[]{:S(2)}, u32[]{:S(2)}) async-start(bf16[8,24,1792]{2,1,0:T(8,128)(2,1)} %bitcast.7), calls=%async_computation.2 | async-start | bytes 1376256 | tf_op jit(solution)/shard_map/all_to_all | solution.py:43
  51.6 36.6 %all-to-all-start.4 = ((bf16[8,24,3584]{2,1,0:T(8,128)(2,1)}), bf16[8,24,3584]{2,1,0:T(8,128)(2,1)S(1)}, u32[]{:S(2)}, u32[]{:S(2)}) async-start(bf16[8,24,3584]{2,1,0:T(8,128)(2,1)} %bitcast.12), calls=%async_computation.4 | async-start | bytes 2752512 | tf_op jit(solution)/shard_map/all_to_all | solution.py:43
  88.2 36.6 %all-to-all-start.1 = ((bf16[8,24,3584]{2,1,0:T(8,128)(2,1)}), bf16[8,24,3584]{2,1,0:T(8,128)(2,1)S(1)}, u32[]{:S(2)}, u32[]{:S(2)}) async-start(bf16[8,24,3584]{2,1,0:T(8,128)(2,1)} %bitcast.108), calls=%async_computation.1 | async-start | bytes 2752512 | tf_op jit(solution)/shard_map/all_to_all | solution.py:43
  125.9 40.9 %all-to-all-start = ((bf16[8,24,3712]{2,1,0:T(8,128)(2,1)}), bf16[8,24,3712]{2,1,0:T(8,128)(2,1)S(1)}, u32[]{:S(2)}, u32[]{:S(2)}) async-start(bf16[8,24,3712]{2,1,0:T(8,128)(2,1)} %bitcast.2), calls=%async_computation | async-start | bytes 2850816 | tf_op jit(solution)/shard_map/all_to_all | solution.py:43
  130.0 33.1 %collective-permute-start.8 = (bf16[192,3584]{1,0:T(8,128)(2,1)S(1)}, bf16[192,3584]{1,0:T(8,128)(2,1)S(1)}, u32[]{:S(2)}, u32[]{:S(2)}) collective-permute-start(bf16[192,3584]{1,0:T(8,128)(2,1)S(1)} %bitcast.98), channel_id=1, source_target_pairs={{0,2},{1,3},{2,0},{3,1},{4,6},{5,7},{6,4},{7,5},{8,10},{9,11},{10,... | collective-permute-start | bytes 4128776 | tf_op jit(solution)/shard_map/ppermute | solution.py:40
  131.6 46.4 %collective-permute-start.4 = (bf16[192,1792]{1,0:T(8,128)(2,1)}, bf16[192,1792]{1,0:T(8,128)(2,1)}, u32[]{:S(2)}, u32[]{:S(2)}) collective-permute-start(bf16[192,1792]{1,0:T(8,128)(2,1)} %bitcast.115), channel_id=1, source_target_pairs={{0,2},{1,3},{2,0},{3,1},{4,6},{5,7},{6,4},{7,5},{8,10},{9,11},{10,... | collective-permute-start | bytes 2064392 | tf_op jit(solution)/shard_map/ppermute | solution.py:40
  132.1 92.4 %collective-permute-start.2 = (bf16[192,3584]{1,0:T(8,128)(2,1)}, bf16[192,3584]{1,0:T(8,128)(2,1)}, u32[]{:S(2)}, u32[]{:S(2)}) collective-permute-start(bf16[192,3584]{1,0:T(8,128)(2,1)} %bitcast.104), channel_id=1, source_target_pairs={{0,2},{1,3},{2,0},{3,1},{4,6},{5,7},{6,4},{7,5},{8,10},{9,11},{10,... | collective-permute-start | bytes 4128776 | tf_op jit(solution)/shard_map/ppermute | solution.py:40
  165.3 92.3 %collective-permute-start.9 = (bf16[384,3584]{1,0:T(8,128)(2,1)}, bf16[384,3584]{1,0:T(8,128)(2,1)}, u32[]{:S(2)}, u32[]{:S(2)}) collective-permute-start(bf16[384,3584]{1,0:T(8,128)(2,1)} %pad_maximum_fusion.8), channel_id=1, source_target_pairs={{0,1},{1,0},{2,3},{3,2},{4,5},{5,4},{6,7},{7,6},{8,9},{9,8},{10,11... | collective-permute-start | bytes 8257544 | tf_op jit(solution)/shard_map/ppermute | solution.py:40
  165.3 57.0 %collective-permute-start.6 = (bf16[192,1792]{1,0:T(8,128)(2,1)S(1)}, bf16[192,1792]{1,0:T(8,128)(2,1)}, u32[]{:S(2)}, u32[]{:S(2)}) collective-permute-start(bf16[192,1792]{1,0:T(8,128)(2,1)S(1)} %bitcast.111), channel_id=1, source_target_pairs={{0,2},{1,3},{2,0},{3,1},{4,6},{5,7},{6,4},{7,5},{8,10},{9,11},{10,... | collective-permute-start | bytes 2064392 | tf_op jit(solution)/shard_map/ppermute | solution.py:40
  166.8 84.6 %collective-permute-start = (bf16[192,3712]{1,0:T(8,128)(2,1)S(1)}, bf16[192,3712]{1,0:T(8,128)(2,1)S(1)}, u32[]{:S(2)}, u32[]{:S(2)}) collective-permute-start(bf16[192,3712]{1,0:T(8,128)(2,1)S(1)} %bitcast.89), channel_id=1, source_target_pairs={{0,2},{1,3},{2,0},{3,1},{4,6},{5,7},{6,4},{7,5},{8,10},{9,11},{10,... | collective-permute-start | bytes 4276232 | tf_op jit(solution)/shard_map/ppermute | solution.py:40
  179.4 72.3 %collective-permute-start.5 = (bf16[384,1792]{1,0:T(8,128)(2,1)S(1)}, bf16[384,1792]{1,0:T(8,128)(2,1)S(1)}, u32[]{:S(2)}, u32[]{:S(2)}) collective-permute-start(bf16[384,1792]{1,0:T(8,128)(2,1)S(1)} %pad_maximum_fusion.14), channel_id=1, source_target_pairs={{0,1},{1,0},{2,3},{3,2},{4,5},{5,4},{6,7},{7,6},{8,9},{9,8},{10,11... | collective-permute-start | bytes 4128776 | tf_op jit(solution)/shard_map/ppermute | solution.py:40
  224.5 66.4 %collective-permute-start.7 = (bf16[384,1792]{1,0:T(8,128)(2,1)}, bf16[384,1792]{1,0:T(8,128)(2,1)}, u32[]{:S(2)}, u32[]{:S(2)}) collective-permute-start(bf16[384,1792]{1,0:T(8,128)(2,1)} %pad_maximum_fusion.15), channel_id=1, source_target_pairs={{0,1},{1,0},{2,3},{3,2},{4,5},{5,4},{6,7},{7,6},{8,9},{9,8},{10,11... | collective-permute-start | bytes 4128776 | tf_op jit(solution)/shard_map/ppermute | solution.py:40
  226.1 45.3 %collective-permute-start.3 = (bf16[384,3584]{1,0:T(8,128)(2,1)S(1)}, bf16[384,3584]{1,0:T(8,128)(2,1)}, u32[]{:S(2)}, u32[]{:S(2)}) collective-permute-start(bf16[384,3584]{1,0:T(8,128)(2,1)S(1)} %pad_maximum_fusion.5), channel_id=1, source_target_pairs={{0,1},{1,0},{2,3},{3,2},{4,5},{5,4},{6,7},{7,6},{8,9},{9,8},{10,11... | collective-permute-start | bytes 8257544 | tf_op jit(solution)/shard_map/ppermute | solution.py:40
  251.7 26.1 %collective-permute-start.1 = (bf16[384,3712]{1,0:T(8,128)(2,1)S(1)}, bf16[384,3712]{1,0:T(8,128)(2,1)S(1)}, u32[]{:S(2)}, u32[]{:S(2)}) collective-permute-start(bf16[384,3712]{1,0:T(8,128)(2,1)S(1)} %pad_maximum_fusion.4), channel_id=1, source_target_pairs={{0,1},{1,0},{2,3},{3,2},{4,5},{5,4},{6,7},{7,6},{8,9},{9,8},{10,11... | collective-permute-start | bytes 8552456 | tf_op jit(solution)/shard_map/ppermute | solution.py:40
  315.3 100.4 %collective-permute-start.16 = (bf16[384,1920]{1,0:T(8,128)(2,1)}, bf16[384,1920]{1,0:T(8,128)(2,1)}, u32[]{:S(2)}, u32[]{:S(2)}) collective-permute-start(bf16[384,1920]{1,0:T(8,128)(2,1)} %pad_maximum_fusion.12), channel_id=1, source_target_pairs={{0,1},{1,0},{2,3},{3,2},{4,5},{5,4},{6,7},{7,6},{8,9},{9,8},{10,11... | collective-permute-start | bytes 4423688 | tf_op jit(solution)/shard_map/ppermute | solution.py:40
  319.3 40.6 %collective-permute-start.14 = (bf16[384,1792]{1,0:T(8,128)(2,1)}, bf16[384,1792]{1,0:T(8,128)(2,1)}, u32[]{:S(2)}, u32[]{:S(2)}) collective-permute-start(bf16[384,1792]{1,0:T(8,128)(2,1)} %split.73), channel_id=1, source_target_pairs={{0,1},{1,0},{2,3},{3,2},{4,5},{5,4},{6,7},{7,6},{8,9},{9,8},{10,11... | collective-permute-start | bytes 4128776 | tf_op jit(solution)/shard_map/ppermute | solution.py:40
  323.1 47.4 %collective-permute-start.12 = (bf16[384,1792]{1,0:T(8,128)(2,1)}, bf16[384,1792]{1,0:T(8,128)(2,1)}, u32[]{:S(2)}, u32[]{:S(2)}) collective-permute-start(bf16[384,1792]{1,0:T(8,128)(2,1)} %split.69), channel_id=1, source_target_pairs={{0,1},{1,0},{2,3},{3,2},{4,5},{5,4},{6,7},{7,6},{8,9},{9,8},{10,11... | collective-permute-start | bytes 4128776 | tf_op jit(solution)/shard_map/ppermute | solution.py:40
  327.9 67.5 %collective-permute-start.10 = (bf16[384,1792]{1,0:T(8,128)(2,1)}, bf16[384,1792]{1,0:T(8,128)(2,1)}, u32[]{:S(2)}, u32[]{:S(2)}) collective-permute-start(bf16[384,1792]{1,0:T(8,128)(2,1)} %split.65), channel_id=1, source_target_pairs={{0,1},{1,0},{2,3},{3,2},{4,5},{5,4},{6,7},{7,6},{8,9},{9,8},{10,11... | collective-permute-start | bytes 4128776 | tf_op jit(solution)/shard_map/ppermute | solution.py:40
  374.2 26.5 %collective-permute-start.13 = (bf16[192,1792]{1,0:T(8,128)(2,1)}, bf16[192,1792]{1,0:T(8,128)(2,1)}, u32[]{:S(2)}, u32[]{:S(2)}) collective-permute-start(bf16[192,1792]{1,0:T(8,128)(2,1)} %split.71), channel_id=1, source_target_pairs={{0,2},{1,3},{2,0},{3,1},{4,6},{5,7},{6,4},{7,5},{8,10},{9,11},{10,... | collective-permute-start | bytes 2064392 | tf_op jit(solution)/shard_map/ppermute | solution.py:40
  381.5 23.2 %all-to-all-start.7 = ((bf16[8,24,1792]{2,1,0:T(8,128)(2,1)}), bf16[8,24,1792]{2,1,0:T(8,128)(2,1)}, u32[]{:S(2)}, u32[]{:S(2)}) async-start(bf16[8,24,1792]{2,1,0:T(8,128)(2,1)} %bitcast.121), calls=%async_computation.7 | async-start | bytes 1376256 | tf_op jit(solution)/shard_map/all_to_all | solution.py:55
  399.3 21.9 %collective-permute-start.11 = (bf16[192,1792]{1,0:T(8,128)(2,1)}, bf16[192,1792]{1,0:T(8,128)(2,1)}, u32[]{:S(2)}, u32[]{:S(2)}) collective-permute-start(bf16[192,1792]{1,0:T(8,128)(2,1)} %split.67), channel_id=1, source_target_pairs={{0,2},{1,3},{2,0},{3,1},{4,6},{5,7},{6,4},{7,5},{8,10},{9,11},{10,... | collective-permute-start | bytes 2064392 | tf_op jit(solution)/shard_map/ppermute | solution.py:40
  426.4 21.8 %all-to-all-start.5 = ((bf16[8,24,1792]{2,1,0:T(8,128)(2,1)}), bf16[8,24,1792]{2,1,0:T(8,128)(2,1)S(1)}, u32[]{:S(2)}, u32[]{:S(2)}) async-start(bf16[8,24,1792]{2,1,0:T(8,128)(2,1)} %bitcast.19), calls=%async_computation.5 | async-start | bytes 1376256 | tf_op jit(solution)/shard_map/all_to_all | solution.py:55
  448.2 22.9 %all-to-all-start.8 = ((bf16[8,24,1920]{2,1,0:T(8,128)(2,1)}), bf16[8,24,1920]{2,1,0:T(8,128)(2,1)S(1)}, u32[]{:S(2)}, u32[]{:S(2)}) async-start(bf16[8,24,1920]{2,1,0:T(8,128)(2,1)} %bitcast.31), calls=%async_computation.8 | async-start | bytes 1474560 | tf_op jit(solution)/shard_map/all_to_all | solution.py:55
  (48 other events, 933.2 us)
